TPU v7x, 256 devices: a whole 4x4x8 slice. The times are simulated.
256 devices in a mesh: gx: 16 (over z_hi, y), gy: 16 (over z_lo, x, core).
Axes of the slice: x: 4, y: 4, z: 8 (z_hi: 4, z_lo: 2; z = z_hi * 2 + z_lo), core: 2. Of those that a mesh axis runs over, the one named last changes fastest.
Arguments:
- snapshot: float32 [8, 512, 512, 128], P(None, 'gx', 'gy'), may hold values from -20 to 20
- start_factor: float32 [512, 128], replicated, may hold values from -0.25 to 0.25
Outputs:
- factor: float32 [512, 128], replicated
- core: float32 [128, 8, 512, 128], P('gx', None, 'gy')
All inputs are finite; a program needn't handle non-finite values.
Results may differ from a plain program's by a relative error of at most 0.00018.
Values sent between devices are 32-bit elements; how exact they have to be, the bound alone decides.
A program may use at most 64 MiB of HBM per device.

v0:
```python
import math

import jax
import jax.numpy as jnp
from jax import lax
from jax.sharding import PartitionSpec as P

ITERS = 2


def on_device(snapshot, start_factor):
    rows_local = snapshot.shape[1]
    unfolded = lax.all_to_all(snapshot, "gx", split_axis=2, concat_axis=1, tiled=True)
    partial_gram = jnp.einsum("vabc,vdbc->ad", unfolded, unfolded, precision=lax.Precision.HIGHEST)
    gram = lax.psum(partial_gram, ("gx", "gy"))
    basis = start_factor
    for step in range(ITERS):
        image = jnp.dot(gram, basis, precision=lax.Precision.HIGHEST)
        small = jnp.dot(image.T, image, precision=lax.Precision.HIGHEST)
        lower = jnp.linalg.cholesky(small)
        basis = jax.scipy.linalg.solve_triangular(lower, image.T, lower=True).T
    factor = basis * math.sqrt(basis.shape[0])
    own_rows = lax.dynamic_slice_in_dim(basis, lax.axis_index("gx") * rows_local, rows_local, 0)
    core = lax.psum_scatter(
        jnp.einsum("ar,vabc->rvbc", own_rows, snapshot, precision=lax.Precision.HIGHEST),
        "gx",
        scatter_dimension=0,
        tiled=True,
    )
    return (factor, core)


def solution(mesh):
    placed = (P(None, "gx", "gy", None), P())
    return jax.shard_map(
        on_device,
        mesh=mesh,
        in_specs=placed,
        out_specs=(P(), P("gx", None, "gy", None)),
        check_vma=False,
    )
```

profile of v0, /device:TPU:1, one launch (start us, length us, event | category | flops | bytes accessed | tf_op | source)
XLA Modules:
  0.0 667.8 jit_solution(5195511991209100175)
XLA Ops:
  7.2 0.0 copy-start
  7.2 0.0 all-reduce.2.cloned.1.call-start
  7.2 4.7 copy.11
  11.9 106.0 %all_to_all.18 = f32[8,32,32,128]{3,1,0,2:T(8,128)S(1)} all-to-all(f32[8,32,32,128]{3,1,0,2:T(8,128)S(1)} %copy.11), channel_id=1, replica_groups=mesh['gx'=16,'gy'=16] {'gx'}, dimensions={2} | all-to-all | bytes 8388608 | tf_op jit(solution)/shard_map/all_to_all | solution.py:13
  117.9 0.6 copy.12
  118.5 7.9 %convolution_bitcast_fusion = f32[512,512]{1,0:T(8,128)} fusion(f32[8,512,2,128]{3,1,0,2:T(8,128)S(1)} %bitcast.47), kind=kOutput, calls=%fused_computation.2 | convolution fusion | flops 6442450944 | bytes 5242880 | tf_op jit(solution)/shard_map/vabc,vdbc->ad/dot_general | solution.py:14
  126.4 0.0 all-reduce.2.cloned.1.call-update
  126.4 0.2 reduce-scatter.2.cloned.1.call-start
  126.7 252.9 %all-reduce.2.cloned.1.call-done = f32[512,512]{1,0:T(8,128)} async-done(((f32[512,512]{1,0:T(8,128)}), f32[512,512]{1,0:T(8,128)}) %all-reduce.2.cloned.1.call-update) | async-done | bytes 1048592 | tf_op jit(solution)/shard_map/psum | solution.py:15
  379.6 0.0 copy-done
  379.6 2.2 fusion.17
  381.8 0.6 fusion.18
  382.4 0.1 copy.13
  382.5 11.7 %cholesky.44 = f32[128,128]{1,0:T(8,128)S(1)} custom-call(f32[128,128]{1,0:T(8,128)S(1)} %fusion.12), custom_call_target="Cholesky" | custom-call | tf_op jit(solution)/shard_map/jit(cholesky)/cholesky | solution.py:20
  394.3 0.6 compare_reduce_fusion.1
  394.9 0.7 fusion.6
  395.6 9.8 %custom-call.6 = f32[1,128,128]{1,2,0:T(8,128)S(1)} custom-call(f32[1,128,128]{2,1,0:T(8,128)S(1)} %fusion.6), custom_call_target="InvertDiagBlocksLowerTriangular" | custom-call | tf_op jit(solution)/shard_map/jit(_solve_triangular)/triangular_solve | solution.py:21
  405.4 0.4 fusion.4
  405.8 2.2 fusion.19
  408.1 0.6 fusion.20
  408.7 0.1 copy.14
  408.8 11.9 %cholesky.55 = f32[128,128]{1,0:T(8,128)S(1)} custom-call(f32[128,128]{1,0:T(8,128)S(1)} %fusion.10), custom_call_target="Cholesky" | custom-call | tf_op jit(solution)/shard_map/jit(cholesky)/cholesky | solution.py:20
  420.7 0.6 compare_reduce_fusion
  421.3 0.7 fusion.7
  422.0 9.8 %custom-call.7 = f32[1,128,128]{1,2,0:T(8,128)S(1)} custom-call(f32[1,128,128]{2,1,0:T(8,128)S(1)} %fusion.7), custom_call_target="InvertDiagBlocksLowerTriangular" | custom-call | tf_op jit(solution)/shard_map/jit(_solve_triangular)/triangular_solve | solution.py:21
  431.8 0.4 fusion.2
  432.2 19.1 %fusion = f32[128,8,32,128]{3,0,2,1:T(8,128)} fusion(f32[8,32,32,128]{3,2,1,0:T(8,128)} %param.5, f32[128,512]{1,0:T(8,128)S(1)} %fusion.2, s32[]{:T(128)S(6)} %select_n.6), kind=kOutput, calls=%fused_computation | convolution fusion | flops 1610612736 | bytes 21037060 | tf_op jit(solution)/shard_map/ar,vabc->rvbc/dot_general | solution.py:25
  451.4 0.0 reduce-scatter.2.cloned.1.call-update
  451.4 0.8 copy.17
  452.3 206.3 %reduce-scatter.2.cloned.1.call-done = f32[8,8,32,128]{3,0,2,1:T(8,128)} async-done(((f32[128,8,32,128]{3,0,2,1:T(8,128)}), f32[8,8,32,128]{3,0,2,1:T(8,128)}) %reduce-scatter.2.cloned.1.call-update) | async-done | bytes 1048592 | tf_op jit(solution)/shard_map/reduce_scatter | solution.py:24
  658.5 2.4 copy.18
  (5 shorter events, 0.1 us)
Async XLA Ops:
  7.2 372.5 %copy-start = (f32[512,128]{1,0:T(8,128)S(1)}, f32[512,128]{1,0:T(8,128)}, u32[]{:S(2)}) copy-start(f32[512,128]{1,0:T(8,128)} %param.6) | copy-start | bytes 786436
  7.2 372.4 %all-reduce.2.cloned.1.call-start = ((), (), s32[]{:S(2)}) async-start(), calls=%async_computation.2 | async-start | bytes 2097152 | tf_op jit(solution)/shard_map/psum | solution.py:15
  126.4 532.1 %reduce-scatter.2.cloned.1.call-start = ((), (), s32[]{:S(2)}) async-start(), calls=%async_computation.3 | async-start | bytes 17825792 | tf_op jit(solution)/shard_map/reduce_scatter | solution.py:24
Sparse Core Ops, SparseCore 0:
  126.6 253.0 all-reduce.1
  451.5 206.9 reduce-scatter.1
where the time goes:
time: 668 us
  waiting for transfers between devices  459 us (69%)
  blocking collectives  106 us (16%)
  other arithmetic  45.9 us (7%)
  matrix products  33.4 us (5%)
  between operations  14.2 us (2%)
  local copies, waits for them, and re-layouts  8.69 us (1%)
    psum x1, waiting for transfers between devices, on_device(): gram = lax.psum(partial_gram, ('gx', 'gy'))  253 us
    reduce_scatter x1, waiting for transfers between devices, on_device(): lax.psum_scatter(jnp.einsum('ar,vabc->rvbc', own_rows, snapshot, precisio...  206 us
    all_to_all x1, blocking collectives, on_device(): lax.all_to_all(snapshot, 'gx', split_axis=2, concat_axis=1, tiled=True)  106 us
    another operation x6, other arithmetic, on_device(): lower = jnp.linalg.cholesky(small)  24.9 us
    another operation x4, other arithmetic, on_device(): basis = jax.scipy.linalg.solve_triangular(lower, image.T, lower=True).T  20.9 us
    dot_general x1, matrix products, on_device(): jnp.einsum('ar,vabc->rvbc', own_rows, snapshot, precision=lax.Precision.H...  19.1 us
  transfers between devices with their start and end apart: 2, of which 2 were waited for; matrix products, arithmetic and copies ran while one was open for 0% of the time, Pallas kernels for 0%

commit v1 on v0

v1 whole, which is shorter than its diff:
```python
import functools
import math

import jax
import jax.numpy as jnp
from jax import lax
from jax.experimental import pallas as pl
from jax.experimental.pallas import tpu as pltpu
from jax.sharding import PartitionSpec as P

ITERS = 2
MESH = pl.DeviceIdType.MESH
HIGHEST = lax.Precision.HIGHEST
F32, BF16 = jnp.float32, jnp.bfloat16

GX_OFFSETS = [(dz, dy) for dz in range(4) for dy in range(4) if dz or dy]
XY_OFFSETS = [(dx, dy) for dx in range(4) for dy in range(4) if dx or dy]
BLOCKS = [(i, j) for i in range(4) for j in range(i + 1)]
SLICE = 5


def dot(a, b, contract, precision=None):
    return lax.dot_general(a, b, ((contract[:1], contract[1:]), ((), ())), precision=precision, preferred_element_type=F32)


def split(x):
    hi = x.astype(BF16)
    return hi, (x - hi.astype(F32)).astype(BF16)


def dot3(a, b, contract):
    return dot(a[0], b[0], contract) + (dot(a[0], b[1], contract) + dot(a[1], b[0], contract))


def place():
    gx, gy = lax.axis_index("gx"), lax.axis_index("gy")
    return gx // 4, gx % 4, gy // 8, (gy // 2) % 4, gy % 2


def gx_peer(dz, dy):
    zh, y, _, _, _ = place()
    return lax.rem(zh + dz, 4) * 4 + lax.rem(y + dy, 4)


def xy_peer(dx, dy):
    zh, y, zl, x, c = place()
    x, y = lax.rem(x + dx, 4), lax.rem(y + dy, 4)
    return x * 4 + y, (zh * 4 + y, zl * 8 + x * 2 + c)


def z_peer(dz):
    zh, y, zl, x, c = place()
    z = lax.rem(zh * 2 + zl + dz, 8)
    return (z // 2 * 4 + y, z % 2 * 8 + x * 2 + c)


def core_peer():
    zh, y, zl, x, c = place()
    return (zh * 4 + y, zl * 8 + x * 2 + 1 - c)


def remote(src, dst, send, recv, device):
    return pltpu.make_async_remote_copy(src_ref=src, dst_ref=dst, send_sem=send, recv_sem=recv, device_id=device, device_id_type=MESH)


def gram_kernel(
    snap, gram, cells_out, cells, high, low, partial, core_buf, part, xy_buf, z_own, z_buf, done,
    local_sem, out_sem, send_sem, recv_sem, csend, crecv, xsend, xrecv, zsend, zrecv, gsend, grecv, fsend, frecv,
):
    gx, gy = lax.axis_index("gx"), lax.axis_index("gy")
    zh, y, zl, x, c = place()
    z = zh * 2 + zl
    barrier = pltpu.get_barrier_semaphore()
    for dz, dy in GX_OFFSETS:
        pl.semaphore_signal(barrier, inc=1, device_id=(gx_peer(dz, dy), gy), device_id_type=MESH)
    for dx, dy in XY_OFFSETS:
        if dx:
            pl.semaphore_signal(barrier, inc=1, device_id=xy_peer(dx, dy)[1], device_id_type=MESH)
    for dz in range(1, 8, 2):
        pl.semaphore_signal(barrier, inc=1, device_id=z_peer(dz), device_id_type=MESH)
    pl.semaphore_signal(barrier, inc=1, device_id=core_peer(), device_id_type=MESH)

    def source(home, h):
        return snap.at[home // 2, :, pl.ds(pl.multiple_of(home % 2 * 16 + h * 8, 8), 8), :]

    own_rows = pl.ds(pl.multiple_of(gx * 32, 32), 32)
    own = [pltpu.make_async_copy(source(gx, h), cells.at[h, own_rows], local_sem.at[h]) for h in range(2)]
    for copy in own:
        copy.start()
    pl.semaphore_wait(barrier, 15 + 12 + 4 + 1)
    moves = []
    for h in range(2):
        for n, (dz, dy) in enumerate(GX_OFFSETS):
            home = gx_peer(dz, dy)
            moves.append(remote(source(home, h), cells.at[h, own_rows], send_sem.at[h * 15 + n], recv_sem.at[h * 15 + n], (home, gy)))
            moves[-1].start()

    flat = cells.reshape(2 * 512 * 8, 128)
    for h in range(2):
        own[h].wait()
        for move in moves[h * 15 : h * 15 + 15]:
            move.wait_recv()
        for b in range(8):
            for q in range(4):
                rows = flat[pl.ds((h * 512 + q * 128) * 8 + b, 128, stride=8), :]
                hi, lo = split(rows)
                high[pl.ds(q * 128, 128), pl.ds(b * 128, 128)] = hi
                low[pl.ds(q * 128, 128), pl.ds(b * 128, 128)] = lo
        pltpu.make_async_copy(cells.at[h], cells_out.at[h], out_sem.at[h]).start()
        for first, start in ((0, 0), (2, 256)):
            rows, cols = pl.ds(start, 512 - start), pl.ds(start, 256)
            term = dot3((high[rows, :], low[rows, :]), (high[cols, :], low[cols, :]), (1, 1))
            for n, (i, j) in enumerate(BLOCKS):
                if j in (first, first + 1):
                    block = term[i * 128 - start : i * 128 - start + 128, (j - first) * 128 : (j - first) * 128 + 128]
                    if h:
                        block = block + partial[pl.ds(n * 128, 128), :]
                    partial[pl.ds(n * 128, 128), :] = block

    half = 80 * 8
    mine, other = pl.ds(pl.multiple_of(c * half, half), half), pl.ds(pl.multiple_of((1 - c) * half, half), half)
    swap = remote(partial.at[other], core_buf, csend.at[0], crecv.at[0], core_peer())
    swap.start()
    swap.wait_recv()
    part[...] = partial[mine, :] + core_buf[...]

    size = SLICE * 8
    me = x * 4 + y
    outs = []
    for n, (dx, dy) in enumerate(XY_OFFSETS):
        q, device = xy_peer(dx, dy)
        outs.append(remote(part.at[pl.ds(pl.multiple_of(q * size, size), size)], xy_buf.at[me], xsend.at[n], xrecv.at[n], device))
        outs[-1].start()
    xy_buf[me] = part[pl.ds(pl.multiple_of(me * size, size), size), :]
    for move in outs:
        move.wait_recv()
    total = xy_buf[0]
    for q in range(1, 16):
        total = total + xy_buf[q]
    z_own[...] = total
    z_buf[z] = total

    passes = []
    for dz in range(1, 8):
        passes.append(remote(z_own, z_buf.at[z], zsend.at[dz - 1], zrecv.at[dz - 1], z_peer(dz)))
        passes[-1].start()
    for move in passes:
        move.wait_recv()
    total = z_buf[0]
    for q in range(1, 8):
        total = total + z_buf[q]

    def slot(q):
        return pl.ds(pl.multiple_of(c * half + q * size, size), size)

    done[slot(me), :] = total
    gathers, onward = [], []
    for n, (dx, dy) in enumerate(XY_OFFSETS):
        gathers.append(remote(done.at[slot(me)], done.at[slot(me)], gsend.at[n], grecv.at[n], xy_peer(dx, dy)[1]))
        gathers[-1].start()
    for n, (dx, dy) in enumerate([(0, 0)] + XY_OFFSETS):
        if n:
            gathers[n - 1].wait_recv()
        q = lax.rem(x - dx + 4, 4) * 4 + lax.rem(y - dy + 4, 4)
        onward.append(remote(done.at[slot(q)], done.at[slot(q)], fsend.at[n], frecv.at[n], core_peer()))
        onward[-1].start()
    for move in onward:
        move.wait_recv()
    gram[...] = done[...]
    for move in moves + [swap] + outs + passes + gathers + onward:
        move.wait_send()
    for h in range(2):
        pltpu.make_async_copy(cells.at[h], cells_out.at[h], out_sem.at[h]).wait()


def triangular_inverse(small, strips):
    lane = lax.broadcasted_iota(jnp.int32, (8, 128), 1)
    sub = lax.broadcasted_iota(jnp.int32, (8, 128), 0)
    left = [small[8 * s : 8 * s + 8, :] for s in range(16)]
    right = [(lane == sub + 8 * s).astype(F32) for s in range(16)]

    def over_rows(strip, i):
        return jnp.broadcast_to(strip[i : i + 1, :], (8, 128))

    def over_lanes(strip, j):
        return jnp.broadcast_to(strip[:, j : j + 1], (8, 128))

    for k in range(16):
        rows_l = [over_rows(left[k], i) for i in range(8)]
        rows_r = [over_rows(right[k], i) for i in range(8)]
        e = [[over_lanes(rows_l[i], 8 * k + j) for j in range(i + 1)] for i in range(8)]
        columns = {s: [over_lanes(left[s], 8 * k + j) for j in range(8)] for s in range(k + 1, 16)}
        inv = []
        low = [[None] * 8 for _ in range(8)]
        for j in range(8):
            inv.append(lax.rsqrt(e[j][j]))
            for i in range(j + 1, 8):
                low[i][j] = e[i][j] * inv[j]
            for i in range(j + 1, 8):
                for m in range(j + 1, i + 1):
                    e[i][m] = e[i][m] - low[i][j] * low[m][j]

        def forward(rhs):
            out = []
            for j in range(8):
                t = rhs[j]
                for m in range(j):
                    t = t - low[j][m] * out[m]
                out.append(t * inv[j])
            return out

        u, v = forward(rows_l), forward(rows_r)
        strip = v[0]
        for j in range(1, 8):
            strip = jnp.where(sub == j, v[j], strip)
        strips[pl.ds(8 * k, 8), :] = strip
        for s in range(k + 1, 16):
            col = forward(columns[s])
            for m in range(8):
                left[s] = left[s] - col[m] * u[m]
                right[s] = right[s] - col[m] * v[m]


def factor_kernel(packed, start, basis, factor, gram, inverse):
    for n, (i, j) in enumerate(BLOCKS):
        block = packed[pl.ds(n * 128, 128), :]
        gram[pl.ds(i * 128, 128), pl.ds(j * 128, 128)] = block
        if i != j:
            gram[pl.ds(j * 128, 128), pl.ds(i * 128, 128)] = block.T
    basis[...] = start[...]

    def iterate(step, carry):
        image = dot(gram[...], basis[...], (1, 0), HIGHEST)
        small = dot(image, image, (0, 0), HIGHEST)
        triangular_inverse(small, inverse)
        basis[...] = dot(image, inverse[...], (1, 1), HIGHEST)
        return carry

    lax.fori_loop(0, ITERS, iterate, 0)
    factor[...] = basis[...] * math.sqrt(512)


def core_kernel(cells_in, basis, core, cells, stage, in_sem, own_sem, send_sem, recv_sem):
    gx, gy = lax.axis_index("gx"), lax.axis_index("gy")
    barrier = pltpu.get_barrier_semaphore()
    for dz, dy in GX_OFFSETS:
        pl.semaphore_signal(barrier, inc=1, device_id=(gx_peer(dz, dy), gy), device_id_type=MESH)
    loads = [pltpu.make_async_copy(cells_in.at[h], cells.at[h], in_sem.at[h]) for h in range(2)]
    for load in loads:
        load.start()
    flat = cells.reshape(2 * 512 * 8, 128)
    staged = stage.reshape(2 * 128 * 8, 128)
    weights = split(basis[...].T)
    moves = []
    for h in range(2):
        loads[h].wait()
        for b in range(8):
            rows = split(flat[pl.ds(h * 4096 + b, 512, stride=8), :])
            staged[pl.ds(h * 1024 + b, 128, stride=8), :] = dot3(weights, rows, (1, 0))
        if h == 0:
            pl.semaphore_wait(barrier, 15)
        cells_at = pl.ds(pl.multiple_of(gx % 2 * 16 + h * 8, 8), 8)
        for n, (dz, dy) in enumerate(GX_OFFSETS):
            home = gx_peer(dz, dy)
            ranks = pl.ds(pl.multiple_of(home * 8, 8), 8)
            moves.append(remote(stage.at[h, ranks], core.at[:, gx // 2, cells_at, :], send_sem.at[h * 15 + n], recv_sem.at[h * 15 + n], (home, gy)))
            moves[-1].start()
        own = pl.ds(pl.multiple_of(gx * 8, 8), 8)
        pltpu.make_async_copy(stage.at[h, own], core.at[:, gx // 2, cells_at, :], own_sem.at[h]).start()
    for move in moves:
        move.wait()
    for h in range(2):
        cells_at = pl.ds(pl.multiple_of(gx % 2 * 16 + h * 8, 8), 8)
        own = pl.ds(pl.multiple_of(gx * 8, 8), 8)
        pltpu.make_async_copy(stage.at[h, own], core.at[:, gx // 2, cells_at, :], own_sem.at[h]).wait()


VMEM = pl.BlockSpec(memory_space=pltpu.VMEM)
ANY = pl.BlockSpec(memory_space=pl.ANY)
DMA = pltpu.SemaphoreType.DMA
LIMIT = 48 * 2**20


def gram_call(snapshot):
    size = SLICE * 8
    return pl.pallas_call(
        gram_kernel,
        out_shape=(jax.ShapeDtypeStruct((1280, 128), F32), jax.ShapeDtypeStruct((2, 512, 8, 128), F32)),
        in_specs=[ANY],
        out_specs=(VMEM, ANY),
        scratch_shapes=[
            pltpu.VMEM((2, 512, 8, 128), F32),
            pltpu.VMEM((512, 1024), BF16),
            pltpu.VMEM((512, 1024), BF16),
            pltpu.VMEM((1280, 128), F32),
            pltpu.VMEM((640, 128), F32),
            pltpu.VMEM((640, 128), F32),
            pltpu.VMEM((16, size, 128), F32),
            pltpu.VMEM((size, 128), F32),
            pltpu.VMEM((8, size, 128), F32),
            pltpu.VMEM((1280, 128), F32),
            DMA((2,)), DMA((2,)), DMA((30,)), DMA((30,)), DMA((1,)), DMA((1,)), DMA((15,)), DMA((15,)),
            DMA((7,)), DMA((7,)), DMA((15,)), DMA((15,)), DMA((16,)), DMA((16,)),
        ],
        compiler_params=pltpu.CompilerParams(collective_id=0, has_side_effects=True, vmem_limit_bytes=LIMIT),
        name="gather_and_gram",
    )(snapshot)


def factor_call(packed, start):
    shape = jax.ShapeDtypeStruct((512, 128), F32)
    return pl.pallas_call(
        factor_kernel,
        out_shape=(shape, shape),
        in_specs=[VMEM, VMEM],
        out_specs=(VMEM, VMEM),
        scratch_shapes=[pltpu.VMEM((512, 512), F32), pltpu.VMEM((128, 128), F32)],
        compiler_params=pltpu.CompilerParams(vmem_limit_bytes=LIMIT),
        name="factorize",
    )(packed, start)


def core_call(cells, basis):
    return pl.pallas_call(
        core_kernel,
        out_shape=jax.ShapeDtypeStruct((8, 8, 32, 128), F32),
        in_specs=[ANY, VMEM],
        out_specs=ANY,
        scratch_shapes=[
            pltpu.VMEM((2, 512, 8, 128), F32),
            pltpu.VMEM((2, 128, 8, 128), F32),
            DMA((2,)), DMA((2,)), DMA((30,)), DMA((30,)),
        ],
        compiler_params=pltpu.CompilerParams(collective_id=1, has_side_effects=True, vmem_limit_bytes=LIMIT),
        name="core_and_scatter",
    )(cells, basis)


def on_device(snapshot, start_factor):
    packed, cells = gram_call(snapshot)
    basis, factor = factor_call(packed, start_factor)
    return factor, core_call(cells, basis)


def solution(mesh):
    return jax.shard_map(
        on_device,
        mesh=mesh,
        in_specs=(P(None, "gx", "gy", None), P()),
        out_specs=(P(), P("gx", None, "gy", None)),
        check_vma=False,
    )
```

time: 668 us -> 178 us (0.27)
  waiting for transfers between devices: 459 us -> 0 us
  Pallas kernels: 0 us -> 177 us
  blocking collectives: 106 us -> 0 us
  other arithmetic: 45.9 us -> 0 us
  matrix products: 33.4 us -> 0 us
  between operations: 14.2 us -> 0.66 us
  local copies, waits for them, and re-layouts: 8.69 us -> 0.98 us
    psum x1 -> x0, waiting for transfers between devices: 253 us -> none  [on_device(): gram = lax.psum(partial_gram, ('gx', 'gy'))]
    reduce_scatter x1 -> x0, waiting for transfers between devices: 206 us -> none  [on_device(): lax.psum_scatter(jnp.einsum('ar,vabc->rvbc', own_rows, snapshot, precisio...]
    pallas_call x0 -> x3, Pallas kernels: none -> 177 us  [the longest x1 131 us: gram_call(): pl.pallas_call(gram_kernel, out_shape=(jax.ShapeDtypeStruct((1280, 128),...]
    all_to_all x1 -> x0, blocking collectives: 106 us -> none  [on_device(): lax.all_to_all(snapshot, 'gx', split_axis=2, concat_axis=1, tiled=True)]
    another operation x10 -> x0, other arithmetic: 45.9 us -> none  [the longest x6 24.9 us: on_device(): lower = jnp.linalg.cholesky(small)]
    dot_general x6 -> x0, matrix products: 32.6 us -> none  [the longest x1 19.1 us: on_device(): jnp.einsum('ar,vabc->rvbc', own_rows, snapshot, precision=lax.Precision.H...]
    unnamed x5 -> x3, local copies, waits for them, and re-layouts: 7.9 us -> 0.98 us
  transfers between devices with their start and end apart: 2 -> 0, of which waited for: 2 -> 0; matrix products, arithmetic and copies ran while one was open for 0% -> 0% of each run, Pallas kernels for 0% -> 0%
where the time goes in v1:
time: 178 us
  Pallas kernels  177 us (99%)
    pallas_call x1, Pallas kernels, gram_call(): pl.pallas_call(gram_kernel, out_shape=(jax.ShapeDtypeStruct((1280, 128),...  131 us
    pallas_call x1, Pallas kernels, core_call(): pl.pallas_call(core_kernel, out_shape=jax.ShapeDtypeStruct((8, 8, 32, 128...  30.6 us
    pallas_call x1, Pallas kernels, factor_call(): pl.pallas_call(factor_kernel, out_shape=(shape, shape), in_specs=[VMEM, V...  14.7 us

profile of v1, /device:TPU:1, one launch (start us, length us, event | category | flops | bytes accessed | tf_op | source)
XLA Modules:
  0.0 178.4 jit_solution(14110259587873395641)
XLA Ops:
  0.6 0.0 copy-start
  0.6 131.4 %gather_and_gram.1 = (f32[1280,128]{1,0:T(8,128)S(1)}, f32[2,512,8,128]{3,2,1,0:T(8,128)S(1)}) custom-call(f32[8,32,32,128]{3,2,1,0:T(8,128)} %snap.1), custom_call_target="tpu_custom_call" | custom-call | tf_op jit(solution)/shard_map/gather_and_gram/pallas_call | solution.py:286
  132.0 0.0 copy-done
  132.1 14.7 %factorize.1 = (f32[512,128]{1,0:T(8,128)S(1)}, f32[512,128]{1,0:T(8,128)}) custom-call(f32[1280,128]{1,0:T(8,128)S(1)} %get-tuple-element.6.packed, f32[512,128]{1,0:T(8,128)S(1)} %copy-done), custom_call_target="tpu_custom_call" | custom-call | tf_op jit(solution)/shard_map/factorize/pallas_call | solution.py:312
  146.8 30.6 %core_and_scatter.1 = f32[8,8,32,128]{3,2,1,0:T(8,128)S(1)} custom-call(f32[2,512,8,128]{3,2,1,0:T(8,128)S(1)} %get-tuple-element.8.cells_in, f32[512,128]{1,0:T(8,128)S(1)} %get-tuple-element.9.basis), custom_call_target="tpu_custom_call" | custom-call | tf_op jit(solution)/shard_map/core_and_scatter/pallas_call | solution.py:324
  177.4 1.0 copy.5
Async XLA Ops:
  0.6 131.4 %copy-start = (f32[512,128]{1,0:T(8,128)S(1)}, f32[512,128]{1,0:T(8,128)}, u32[]{:S(2)}) copy-start(f32[512,128]{1,0:T(8,128)} %start.1) | copy-start | bytes 786436

commit v2 on v0

v2 whole, which is shorter than its diff:
```python
import functools
import math

import jax
import jax.numpy as jnp
from jax import lax
from jax.experimental import pallas as pl
from jax.experimental.pallas import tpu as pltpu
from jax.sharding import PartitionSpec as P

ITERS = 2
MESH = pl.DeviceIdType.MESH
HIGHEST = lax.Precision.HIGHEST
F32, BF16 = jnp.float32, jnp.bfloat16

GX_OFFSETS = [(dz, dy) for dz in (2, 1, 3, 0) for dy in (2, 1, 3, 0) if dz or dy]
XY_OFFSETS = [(dx, dy) for dx in (2, 1, 3, 0) for dy in (2, 1, 3, 0) if dx or dy]
Z_OFFSETS = (4, 3, 5, 2, 6, 1, 7)
BLOCKS = [(i, j) for i in range(4) for j in range(i + 1)]
SLICE = 5
STOP = 9


def dot(a, b, contract, precision=None):
    return lax.dot_general(a, b, ((contract[:1], contract[1:]), ((), ())), precision=precision, preferred_element_type=F32)


def split(x):
    hi = x.astype(BF16)
    return hi, (x - hi.astype(F32)).astype(BF16)


def dot3(a, b, contract):
    return dot(a[0], b[0], contract) + (dot(a[0], b[1], contract) + dot(a[1], b[0], contract))


def place():
    gx, gy = lax.axis_index("gx"), lax.axis_index("gy")
    return gx // 4, gx % 4, gy // 8, (gy // 2) % 4, gy % 2


def gx_peer(dz, dy):
    zh, y, _, _, _ = place()
    return lax.rem(zh + dz, 4) * 4 + lax.rem(y + dy, 4)


def xy_peer(dx, dy):
    zh, y, zl, x, c = place()
    x, y = lax.rem(x + dx, 4), lax.rem(y + dy, 4)
    return x * 4 + y, (zh * 4 + y, zl * 8 + x * 2 + c)


def z_peer(dz):
    zh, y, zl, x, c = place()
    z = lax.rem(zh * 2 + zl + dz, 8)
    return (z // 2 * 4 + y, z % 2 * 8 + x * 2 + c)


def core_peer():
    zh, y, zl, x, c = place()
    return (zh * 4 + y, zl * 8 + x * 2 + 1 - c)


def remote(src, dst, send, recv, device):
    return pltpu.make_async_remote_copy(src_ref=src, dst_ref=dst, send_sem=send, recv_sem=recv, device_id=device, device_id_type=MESH)


def rows_of(index, size):
    return pl.ds(pl.multiple_of(index * size, size), size)


def triangular_inverse(small, strips):
    lane = lax.broadcasted_iota(jnp.int32, (8, 128), 1)
    sub = lax.broadcasted_iota(jnp.int32, (8, 128), 0)
    left = [small[8 * s : 8 * s + 8, :] for s in range(16)]
    right = [(lane == sub + 8 * s).astype(F32) for s in range(16)]

    def over_rows(strip, i):
        return jnp.broadcast_to(strip[i : i + 1, :], (8, 128))

    def over_lanes(strip, j):
        return jnp.broadcast_to(strip[:, j : j + 1], (8, 128))

    for k in range(16):
        rows_l = [over_rows(left[k], i) for i in range(8)]
        rows_r = [over_rows(right[k], i) for i in range(8)]
        e = [[over_lanes(rows_l[i], 8 * k + j) for j in range(i + 1)] for i in range(8)]
        columns = {s: [over_lanes(left[s], 8 * k + j) for j in range(8)] for s in range(k + 1, 16)}
        inv = []
        low = [[None] * 8 for _ in range(8)]
        for j in range(8):
            inv.append(lax.rsqrt(e[j][j]))
            for i in range(j + 1, 8):
                low[i][j] = e[i][j] * inv[j]
            for i in range(j + 1, 8):
                for m in range(j + 1, i + 1):
                    e[i][m] = e[i][m] - low[i][j] * low[m][j]

        def forward(rhs):
            out = []
            for j in range(8):
                t = rhs[j]
                for m in range(j):
                    t = t - low[j][m] * out[m]
                out.append(t * inv[j])
            return out

        u, v = forward(rows_l), forward(rows_r)
        strip = v[0]
        for j in range(1, 8):
            strip = jnp.where(sub == j, v[j], strip)
        strips[pl.ds(8 * k, 8), :] = strip
        for s in range(k + 1, 16):
            col = forward(columns[s])
            for m in range(8):
                left[s] = left[s] - col[m] * u[m]
                right[s] = right[s] - col[m] * v[m]


def kernel(
    snap, start, factor, core,
    cells, high, low, partial, core_buf, part, xy_buf, z_own, z_buf, done, gram, basis, inverse, stage,
    local_sem, send_sem, recv_sem, csend, crecv, xsend, xrecv, zsend, zrecv, gsend, grecv, fsend, frecv,
    bsend, brecv, known,
):
    gx, gy = lax.axis_index("gx"), lax.axis_index("gy")
    zh, y, zl, x, c = place()
    z = zh * 2 + zl

    def source(home, h):
        return snap.at[home // 2, :, pl.ds(pl.multiple_of(home % 2 * 16 + h * 8, 8), 8), :]

    own = [pltpu.make_async_copy(source(gx, h), cells.at[h, rows_of(gx, 32)], local_sem.at[h]) for h in range(2)]
    near = [z_peer(2), z_peer(6), xy_peer(0, 1)[1], xy_peer(0, 3)[1], xy_peer(1, 0)[1], xy_peer(3, 0)[1]]
    barrier = pltpu.get_barrier_semaphore()
    for device in near + [z_peer(1), z_peer(7), core_peer()]:
        pl.semaphore_signal(barrier, inc=1, device_id=device, device_id_type=MESH)
    for copy in own:
        copy.start()
    pl.semaphore_wait(barrier, 9)
    moves = {}

    def send(h, n):
        dz, dy = GX_OFFSETS[n]
        home = gx_peer(dz, dy)
        moves[h, n] = remote(source(home, h), cells.at[h, rows_of(gx, 32)], send_sem.at[h * 15 + n], recv_sem.at[h * 15 + n], (home, gy))
        moves[h, n].start()

    for steps in range(1, 5):
        if steps < 4:
            for device in near:
                pl.semaphore_signal(known.at[steps - 1], inc=1, device_id=device, device_id_type=MESH)
        for n, (dz, dy) in enumerate(GX_OFFSETS):
            if min(dz, 4 - dz) + min(dy, 4 - dy) == steps:
                send(0, n)
        if steps < 4:
            pl.semaphore_wait(known.at[steps - 1], 6)
    for n in range(15):
        send(1, n)
    sent = list(moves.values())

    flat = cells.reshape(2 * 512 * 8, 128)

    def convert(h, row):
        for b in range(8):
            rows = flat[pl.ds((h * 512 + row * 32) * 8 + b, 32, stride=8), :]
            hi, lo = split(rows)
            high[h, rows_of(row, 32), pl.ds(b * 128, 128)] = hi
            low[h, rows_of(row, 32), pl.ds(b * 128, 128)] = lo

    for h in range(2):
        own[h].wait()
        if STOP >= 2:
            convert(h, gx)
        if STOP >= 1:
            for n, (dz, dy) in enumerate(GX_OFFSETS):
                moves[h, n].wait_recv()
                if STOP >= 2:
                    convert(h, gx_peer((4 - dz) % 4, (4 - dy) % 4))
        if STOP >= 3:
            for first, at in ((0, 0), (2, 256)):
                rows, cols = pl.ds(at, 512 - at), pl.ds(at, 256)
                term = dot3((high[h, rows, :], low[h, rows, :]), (high[h, cols, :], low[h, cols, :]), (1, 1))
                for n, (i, j) in enumerate(BLOCKS):
                    if j in (first, first + 1):
                        block = term[i * 128 - at : i * 128 - at + 128, (j - first) * 128 : (j - first) * 128 + 128]
                        if h:
                            block = block + partial[pl.ds(n * 128, 128), :]
                        partial[pl.ds(n * 128, 128), :] = block

    half = 80 * 8
    if STOP >= 4:
        swap = remote(partial.at[rows_of(1 - c, half)], core_buf, csend.at[0], crecv.at[0], core_peer())
        swap.start()
        sent.append(swap)
        swap.wait_recv()
        part[...] = partial[rows_of(c, half), :] + core_buf[...]

    size = SLICE * 8
    me = x * 4 + y
    if STOP >= 5:
        outs = []
        for n, (dx, dy) in enumerate(XY_OFFSETS):
            q, device = xy_peer(dx, dy)
            outs.append(remote(part.at[rows_of(q, size)], xy_buf.at[me], xsend.at[n], xrecv.at[n], device))
            outs[-1].start()
        xy_buf[me] = part[rows_of(me, size), :]
        for move in outs:
            move.wait_recv()
        sent += outs
        total = xy_buf[0]
        for q in range(1, 16):
            total = total + xy_buf[q]
        z_own[...] = total
        z_buf[z] = total

    if STOP >= 6:
        passes = []
        for n, dz in enumerate(Z_OFFSETS):
            passes.append(remote(z_own, z_buf.at[z], zsend.at[n], zrecv.at[n], z_peer(dz)))
            passes[-1].start()
        for move in passes:
            move.wait_recv()
        sent += passes
        total = z_buf[0]
        for q in range(1, 8):
            total = total + z_buf[q]

    def slot(q):
        return pl.ds(pl.multiple_of(c * half + q * size, size), size)

    if STOP >= 7:
        done[slot(me), :] = total
        gathers, onward = [], []
        for n, (dx, dy) in enumerate(XY_OFFSETS):
            gathers.append(remote(done.at[slot(me)], done.at[slot(me)], gsend.at[n], grecv.at[n], xy_peer(dx, dy)[1]))
            gathers[-1].start()
        near = [(0, 0)] + [XY_OFFSETS[n] for n in range(14, -1, -1)]
        for n, (dx, dy) in enumerate(near):
            if n:
                gathers[15 - n].wait_recv()
            q = lax.rem(x - dx + 4, 4) * 4 + lax.rem(y - dy + 4, 4)
            onward.append(remote(done.at[slot(q)], done.at[slot(q)], fsend.at[n], frecv.at[n], core_peer()))
            onward[-1].start()
        for move in onward:
            move.wait_recv()
        sent += gathers + onward

    if STOP >= 8:
        for n, (i, j) in enumerate(BLOCKS):
            block = done[pl.ds(n * 128, 128), :]
            gram[pl.ds(i * 128, 128), pl.ds(j * 128, 128)] = block
            if i != j:
                gram[pl.ds(j * 128, 128), pl.ds(i * 128, 128)] = block.T
        basis[...] = start[...]

        def iterate(step, carry):
            image = dot(gram[...], basis[...], (1, 0), HIGHEST)
            small = dot(image, image, (0, 0), HIGHEST)
            triangular_inverse(small, inverse)
            basis[...] = dot(image, inverse[...], (1, 1), HIGHEST)
            return carry

        lax.fori_loop(0, ITERS, iterate, 0)
    factor[...] = basis[...] * math.sqrt(512)

    if STOP >= 9:
        staged = stage.reshape(2 * 128 * 8, 128)
        weights = split(basis[...].T)
        backs = []
        for h in range(2):
            block = dot3(weights, (high[h], low[h]), (1, 0))
            for b in range(8):
                staged[pl.ds(h * 1024 + b, 128, stride=8), :] = block[:, b * 128 : b * 128 + 128]
            at = pl.ds(pl.multiple_of(gx % 2 * 16 + h * 8, 8), 8)
            for n, (dz, dy) in enumerate(GX_OFFSETS):
                home = gx_peer(dz, dy)
                backs.append(remote(stage.at[h, rows_of(home, 8)], core.at[:, gx // 2, at, :], bsend.at[h * 15 + n], brecv.at[h * 15 + n], (home, gy)))
                backs[-1].start()
            core[:, gx // 2, at, :] = stage[h, rows_of(gx, 8)]
        for move in backs:
            move.wait_recv()
        sent += backs
    for move in sent:
        move.wait_send()


VMEM = pl.BlockSpec(memory_space=pltpu.VMEM)
ANY = pl.BlockSpec(memory_space=pl.ANY)
DMA = pltpu.SemaphoreType.DMA


def on_device(snapshot, start_factor):
    size = SLICE * 8
    return pl.pallas_call(
        kernel,
        out_shape=(jax.ShapeDtypeStruct((512, 128), F32), jax.ShapeDtypeStruct((8, 8, 32, 128), F32)),
        in_specs=[ANY, VMEM],
        out_specs=(VMEM, VMEM),
        scratch_shapes=[
            pltpu.VMEM((2, 512, 8, 128), F32),
            pltpu.VMEM((2, 512, 1024), BF16),
            pltpu.VMEM((2, 512, 1024), BF16),
            pltpu.VMEM((1280, 128), F32),
            pltpu.VMEM((640, 128), F32),
            pltpu.VMEM((640, 128), F32),
            pltpu.VMEM((16, size, 128), F32),
            pltpu.VMEM((size, 128), F32),
            pltpu.VMEM((8, size, 128), F32),
            pltpu.VMEM((1280, 128), F32),
            pltpu.VMEM((512, 512), F32),
            pltpu.VMEM((512, 128), F32),
            pltpu.VMEM((128, 128), F32),
            pltpu.VMEM((2, 128, 8, 128), F32),
            DMA((2,)), DMA((30,)), DMA((30,)), DMA((1,)), DMA((1,)), DMA((15,)), DMA((15,)),
            DMA((7,)), DMA((7,)), DMA((15,)), DMA((15,)), DMA((16,)), DMA((16,)),
            DMA((30,)), DMA((30,)), pltpu.SemaphoreType.REGULAR((3,)),
        ],
        compiler_params=pltpu.CompilerParams(collective_id=0, has_side_effects=True, vmem_limit_bytes=48 * 2**20),
        name="hosvd_mode",
    )(snapshot, start_factor)


def solution(mesh):
    return jax.shard_map(
        on_device,
        mesh=mesh,
        in_specs=(P(None, "gx", "gy", None), P()),
        out_specs=(P(), P("gx", None, "gy", None)),
        check_vma=False,
    )
```

time: 668 us -> 172 us (0.26)
  waiting for transfers between devices: 459 us -> 0 us
  Pallas kernels: 0 us -> 166 us
  blocking collectives: 106 us -> 0 us
  other arithmetic: 45.9 us -> 0 us
  matrix products: 33.4 us -> 0 us
  between operations: 14.2 us -> 0.65 us
    psum x1 -> x0, waiting for transfers between devices: 253 us -> none  [on_device(): gram = lax.psum(partial_gram, ('gx', 'gy'))]
    reduce_scatter x1 -> x0, waiting for transfers between devices: 206 us -> none  [on_device(): lax.psum_scatter(jnp.einsum('ar,vabc->rvbc', own_rows, snapshot, precisio...]
    pallas_call x0 -> x1, Pallas kernels: none -> 166 us  [on_device(): pl.pallas_call(kernel, out_shape=(jax.ShapeDtypeStruct((512, 128), F32),...]
    all_to_all x1 -> x0, blocking collectives: 106 us -> none  [on_device(): lax.all_to_all(snapshot, 'gx', split_axis=2, concat_axis=1, tiled=True)]
    another operation x10 -> x0, other arithmetic: 45.9 us -> none  [the longest x6 24.9 us: on_device(): lower = jnp.linalg.cholesky(small)]
    dot_general x6 -> x0, matrix products: 32.6 us -> none  [the longest x1 19.1 us: on_device(): jnp.einsum('ar,vabc->rvbc', own_rows, snapshot, precision=lax.Precision.H...]
  transfers between devices with their start and end apart: 2 -> 0, of which waited for: 2 -> 0; matrix products, arithmetic and copies ran while one was open for 0% -> 0% of each run, Pallas kernels for 0% -> 0%
where the time goes in v2:
time: 172 us
  Pallas kernels  166 us (97%)
  local copies, waits for them, and re-layouts  4.81 us (3%)
    pallas_call x1, Pallas kernels, on_device(): pl.pallas_call(kernel, out_shape=(jax.ShapeDtypeStruct((512, 128), F32),...  166 us
    unnamed x6, local copies, waits for them, and re-layouts  4.81 us

profile of v2, /device:TPU:1, one launch (start us, length us, event | category | flops | bytes accessed | tf_op | source)
XLA Modules:
  0.0 171.7 jit_solution(13364026645826239028)
XLA Ops:
  0.6 0.0 copy-start
  0.6 2.2 %copy-done = f32[8,32,32,128]{3,2,1,0:T(8,128)S(1)} copy-done((f32[8,32,32,128]{3,2,1,0:T(8,128)S(1)}, f32[8,32,32,128]{3,2,1,0:T(8,128)}, u32[]{:S(2)}) %copy-start) | copy-done | bytes 4194328
  2.8 0.0 copy-start.1
  2.8 0.9 copy-done.1
  3.8 166.2 %hosvd_mode.1 = (f32[512,128]{1,0:T(8,128)S(1)}, f32[8,8,32,128]{3,2,1,0:T(8,128)S(1)}) custom-call(f32[8,32,32,128]{3,2,1,0:T(8,128)S(1)} %copy-done, f32[512,128]{1,0:T(8,128)S(1)} %copy-done.1), custom_call_target="tpu_custom_call" | custom-call | tf_op jit(solution)/shard_map/hosvd_mode/pallas_call | solution.py:295
  170.0 0.7 copy.6
  170.7 1.0 copy.7
Async XLA Ops:
  0.6 2.2 %copy-start = (f32[8,32,32,128]{3,2,1,0:T(8,128)S(1)}, f32[8,32,32,128]{3,2,1,0:T(8,128)}, u32[]{:S(2)}) copy-start(f32[8,32,32,128]{3,2,1,0:T(8,128)} %snap.1) | copy-start | bytes 12582916
  2.8 0.9 copy-start.1

commit v3 on v2

--- a/solution.py
+++ b/solution.py
@@ -19,6 +19,7 @@
 BLOCKS = [(i, j) for i in range(4) for j in range(i + 1)]
 SLICE = 5
 STOP = 9
+LIMIT = 50 * 2**20
 
 
 def dot(a, b, contract, precision=None):
@@ -69,11 +70,10 @@
     return pl.ds(pl.multiple_of(index * size, size), size)
 
 
-def triangular_inverse(small, strips):
+def triangular_inverse(small, strips, after=None):
     lane = lax.broadcasted_iota(jnp.int32, (8, 128), 1)
     sub = lax.broadcasted_iota(jnp.int32, (8, 128), 0)
-    left = [small[8 * s : 8 * s + 8, :] for s in range(16)]
-    right = [(lane == sub + 8 * s).astype(F32) for s in range(16)]
+    work = [small[8 * s : 8 * s + 8, :] for s in range(16)]
 
     def over_rows(strip, i):
         return jnp.broadcast_to(strip[i : i + 1, :], (8, 128))
@@ -82,10 +82,10 @@
         return jnp.broadcast_to(strip[:, j : j + 1], (8, 128))
 
     for k in range(16):
-        rows_l = [over_rows(left[k], i) for i in range(8)]
-        rows_r = [over_rows(right[k], i) for i in range(8)]
-        e = [[over_lanes(rows_l[i], 8 * k + j) for j in range(i + 1)] for i in range(8)]
-        columns = {s: [over_lanes(left[s], 8 * k + j) for j in range(8)] for s in range(k + 1, 16)}
+        rows = [over_rows(work[k], i) for i in range(8)]
+        e = [[over_lanes(rows[i], 8 * k + j) for j in range(i + 1)] for i in range(8)]
+        columns = {s: [over_lanes(work[s], 8 * k + j) for j in range(8)] for s in range(k + 1, 16)}
+        inside = (lane >= 8 * k) & (lane < 8 * k + 8)
         inv = []
         low = [[None] * 8 for _ in range(8)]
         for j in range(8):
@@ -105,23 +105,26 @@
                 out.append(t * inv[j])
             return out
 
-        u, v = forward(rows_l), forward(rows_r)
-        strip = v[0]
+        u = forward([jnp.where(inside, (lane == 8 * k + i).astype(F32), rows[i]) for i in range(8)])
+        strip = u[0]
         for j in range(1, 8):
-            strip = jnp.where(sub == j, v[j], strip)
-        strips[pl.ds(8 * k, 8), :] = strip
+            strip = jnp.where(sub == j, u[j], strip)
+        strips[pl.ds(8 * k, 8), :] = jnp.where(lane < 8 * k + 8, strip, 0.0)
         for s in range(k + 1, 16):
             col = forward(columns[s])
+            t = jnp.where(inside, 0.0, work[s])
             for m in range(8):
-                left[s] = left[s] - col[m] * u[m]
-                right[s] = right[s] - col[m] * v[m]
+                t = t - col[m] * u[m]
+            work[s] = t
+        if after and k % 4 == 3:
+            after(k // 4)
 
 
 def kernel(
     snap, start, factor, core,
-    cells, high, low, partial, core_buf, part, xy_buf, z_own, z_buf, done, gram, basis, inverse, stage,
+    cells, high, low, partial, core_buf, part, xy_buf, z_own, z_buf, done, gram, basis, turned, image, inverse, stage,
     local_sem, send_sem, recv_sem, csend, crecv, xsend, xrecv, zsend, zrecv, gsend, grecv, fsend, frecv,
-    bsend, brecv, known,
+    bsend, brecv, known, start_sem,
 ):
     gx, gy = lax.axis_index("gx"), lax.axis_index("gy")
     zh, y, zl, x, c = place()
@@ -135,7 +138,8 @@
     barrier = pltpu.get_barrier_semaphore()
     for device in near + [z_peer(1), z_peer(7), core_peer()]:
         pl.semaphore_signal(barrier, inc=1, device_id=device, device_id_type=MESH)
-    for copy in own:
+    begin = pltpu.make_async_copy(start, basis, start_sem.at[0])
+    for copy in own + [begin]:
         copy.start()
     pl.semaphore_wait(barrier, 9)
     moves = {}
@@ -159,6 +163,8 @@
         send(1, n)
     sent = list(moves.values())
 
+    begin.wait()
+    turned[...] = basis[...].T
     flat = cells.reshape(2 * 512 * 8, 128)
 
     def convert(h, row):
@@ -252,34 +258,49 @@
             gram[pl.ds(i * 128, 128), pl.ds(j * 128, 128)] = block
             if i != j:
                 gram[pl.ds(j * 128, 128), pl.ds(i * 128, 128)] = block.T
-        basis[...] = start[...]
-
-        def iterate(step, carry):
-            image = dot(gram[...], basis[...], (1, 0), HIGHEST)
-            small = dot(image, image, (0, 0), HIGHEST)
-            triangular_inverse(small, inverse)
-            basis[...] = dot(image, inverse[...], (1, 1), HIGHEST)
-            return carry
-
-        lax.fori_loop(0, ITERS, iterate, 0)
-    factor[...] = basis[...] * math.sqrt(512)
-
-    if STOP >= 9:
         staged = stage.reshape(2 * 128 * 8, 128)
-        weights = split(basis[...].T)
         backs = []
+
+        def cells_at(h):
+            return pl.ds(pl.multiple_of(gx % 2 * 16 + h * 8, 8), 8)
+
+        def back(h, home, n, m):
+            backs.append(remote(stage.at[h, rows_of(home, 8)], core.at[:, gx // 2, cells_at(h), :], bsend.at[n], brecv.at[m], (home, gy)))
+            backs[-1].start()
+
+        def ranks_done(r):
+            ranks = pl.ds(32 * r, 32)
+            rows = dot(inverse[ranks, :], image[...], (1, 0), HIGHEST)
+            turned[ranks, :] = rows
+            weights = split(rows)
+            for h in range(2):
+                block = dot3(weights, (high[h], low[h]), (1, 0))
+                for b in range(8):
+                    staged[pl.ds(h * 1024 + r * 256 + b, 32, stride=8), :] = block[:, b * 128 : b * 128 + 128]
+                for dy in (2, 1, 3):
+                    back(h, r * 4 + lax.rem(y + dy, 4), 6 + (h * 4 + r) * 3 + dy - 1, 6 + (h * 4 + zh) * 3 + dy - 1)
+
+        for step in range(ITERS):
+            image[...] = dot(turned[...], gram[...], (1, 0), HIGHEST)
+            small = dot(image[...], image[...], (1, 1), HIGHEST)
+            if step < ITERS - 1:
+                triangular_inverse(small, inverse)
+                turned[...] = dot(inverse[...], image[...], (1, 0), HIGHEST)
+            else:
+                triangular_inverse(small, inverse, ranks_done)
         for h in range(2):
-            block = dot3(weights, (high[h], low[h]), (1, 0))
-            for b in range(8):
-                staged[pl.ds(h * 1024 + b, 128, stride=8), :] = block[:, b * 128 : b * 128 + 128]
-            at = pl.ds(pl.multiple_of(gx % 2 * 16 + h * 8, 8), 8)
-            for n, (dz, dy) in enumerate(GX_OFFSETS):
-                home = gx_peer(dz, dy)
-                backs.append(remote(stage.at[h, rows_of(home, 8)], core.at[:, gx // 2, at, :], bsend.at[h * 15 + n], brecv.at[h * 15 + n], (home, gy)))
-                backs[-1].start()
-            core[:, gx // 2, at, :] = stage[h, rows_of(gx, 8)]
-        for move in backs:
+            for dz in (2, 1, 3):
+                back(h, gx_peer(dz, 0), h * 3 + dz - 1, h * 3 + dz - 1)
+        factor[...] = turned[...].T * math.sqrt(512)
+        for h in range(2):
+            core[:, gx // 2, cells_at(h), :] = stage[h, rows_of(gx, 8)]
+        for move in backs[24:]:
             move.wait_recv()
+        for h in range(2):
+            for source_zh in range(4):
+                for dy in range(1, 4):
+                    m = 6 + (h * 4 + source_zh) * 3 + dy - 1
+                    remote(stage.at[h, rows_of(gx, 8)], core.at[:, gx // 2, cells_at(h), :], bsend.at[m], brecv.at[m], (gx_peer(0, dy), gy)).wait_recv()
         sent += backs
     for move in sent:
         move.wait_send()
@@ -292,10 +313,11 @@
 
 def on_device(snapshot, start_factor):
     size = SLICE * 8
+    outs = (jax.ShapeDtypeStruct((512, 128), F32), jax.ShapeDtypeStruct((8, 8, 32, 128), F32))
     return pl.pallas_call(
         kernel,
-        out_shape=(jax.ShapeDtypeStruct((512, 128), F32), jax.ShapeDtypeStruct((8, 8, 32, 128), F32)),
-        in_specs=[ANY, VMEM],
+        out_shape=outs,
+        in_specs=[ANY, ANY],
         out_specs=(VMEM, VMEM),
         scratch_shapes=[
             pltpu.VMEM((2, 512, 8, 128), F32),
@@ -310,13 +332,15 @@
             pltpu.VMEM((1280, 128), F32),
             pltpu.VMEM((512, 512), F32),
             pltpu.VMEM((512, 128), F32),
+            pltpu.VMEM((128, 512), F32),
+            pltpu.VMEM((128, 512), F32),
             pltpu.VMEM((128, 128), F32),
             pltpu.VMEM((2, 128, 8, 128), F32),
             DMA((2,)), DMA((30,)), DMA((30,)), DMA((1,)), DMA((1,)), DMA((15,)), DMA((15,)),
             DMA((7,)), DMA((7,)), DMA((15,)), DMA((15,)), DMA((16,)), DMA((16,)),
-            DMA((30,)), DMA((30,)), pltpu.SemaphoreType.REGULAR((3,)),
+            DMA((30,)), DMA((30,)), pltpu.SemaphoreType.REGULAR((3,)), DMA((1,)),
         ],
-        compiler_params=pltpu.CompilerParams(collective_id=0, has_side_effects=True, vmem_limit_bytes=48 * 2**20),
+        compiler_params=pltpu.CompilerParams(collective_id=0, has_side_effects=True, vmem_limit_bytes=LIMIT),
         name="hosvd_mode",
     )(snapshot, start_factor)
 

time: 172 us -> 166 us (0.965)
  Pallas kernels: 166 us -> 163 us
  local copies, waits for them, and re-layouts: 4.81 us -> 2.62 us
    pallas_call x1, Pallas kernels: 166 us -> 163 us  [on_device(): pl.pallas_call(kernel, out_shape=outs, in_specs=[ANY, ANY], out_specs=(VM...]
    unnamed x6 -> x4, local copies, waits for them, and re-layouts: 4.81 us -> 2.62 us
where the time goes in v3:
time: 166 us
  Pallas kernels  163 us (98%)
  local copies, waits for them, and re-layouts  2.62 us (2%)
    pallas_call x1, Pallas kernels, on_device(): pl.pallas_call(kernel, out_shape=outs, in_specs=[ANY, ANY], out_specs=(VM...  163 us

profile of v3, /device:TPU:1, one launch (start us, length us, event | category | flops | bytes accessed | tf_op | source)
XLA Modules:
  0.0 166.2 jit_solution(9037594335144549194)
XLA Ops:
  0.6 0.0 copy-start
  0.6 0.9 copy-done
  1.6 163.0 %hosvd_mode.1 = (f32[512,128]{1,0:T(8,128)S(1)}, f32[8,8,32,128]{3,2,1,0:T(8,128)S(1)}) custom-call(f32[8,32,32,128]{3,2,1,0:T(8,128)} %snap.1, f32[512,128]{1,0:T(8,128)S(1)} %copy-done), custom_call_target="tpu_custom_call" | custom-call | tf_op jit(solution)/shard_map/hosvd_mode/pallas_call | solution.py:317
  164.6 0.7 copy.6
  165.3 1.0 copy.7
Async XLA Ops:
  0.6 1.0 copy-start

commit v4 on v3

--- a/solution.py
+++ b/solution.py
@@ -17,6 +17,7 @@
 XY_OFFSETS = [(dx, dy) for dx in (2, 1, 3, 0) for dy in (2, 1, 3, 0) if dx or dy]
 Z_OFFSETS = (4, 3, 5, 2, 6, 1, 7)
 BLOCKS = [(i, j) for i in range(4) for j in range(i + 1)]
+PARTS = [(0, 16), (16, 24)]
 SLICE = 5
 STOP = 9
 LIMIT = 50 * 2**20
@@ -204,53 +205,51 @@
 
     size = SLICE * 8
     me = x * 4 + y
-    if STOP >= 5:
-        outs = []
+    outs, passes, gathers, onward = {}, {}, {}, {}
+    for p, (at, rows) in enumerate(PARTS):
         for n, (dx, dy) in enumerate(XY_OFFSETS):
             q, device = xy_peer(dx, dy)
-            outs.append(remote(part.at[rows_of(q, size)], xy_buf.at[me], xsend.at[n], xrecv.at[n], device))
-            outs[-1].start()
-        xy_buf[me] = part[rows_of(me, size), :]
-        for move in outs:
-            move.wait_recv()
-        sent += outs
-        total = xy_buf[0]
+            piece = part.at[pl.ds(pl.multiple_of(q * size + at, 8), rows)]
+            outs[p, n] = remote(piece, xy_buf.at[me, pl.ds(at, rows)], xsend.at[p * 15 + n], xrecv.at[p * 15 + n], device)
+            outs[p, n].start()
+    xy_buf[me] = part[rows_of(me, size), :]
+    for p, (at, rows) in enumerate(PARTS):
+        for n in range(15):
+            outs[p, n].wait_recv()
+        total = xy_buf[0, pl.ds(at, rows), :]
         for q in range(1, 16):
-            total = total + xy_buf[q]
-        z_own[...] = total
-        z_buf[z] = total
-
-    if STOP >= 6:
-        passes = []
+            total = total + xy_buf[q, pl.ds(at, rows), :]
+        z_buf[z, pl.ds(at, rows), :] = total
+        z_own[pl.ds(at, rows), :] = total
         for n, dz in enumerate(Z_OFFSETS):
-            passes.append(remote(z_own, z_buf.at[z], zsend.at[n], zrecv.at[n], z_peer(dz)))
-            passes[-1].start()
-        for move in passes:
-            move.wait_recv()
-        sent += passes
-        total = z_buf[0]
+            passes[p, n] = remote(z_own.at[pl.ds(at, rows)], z_buf.at[z, pl.ds(at, rows)], zsend.at[p * 7 + n], zrecv.at[p * 7 + n], z_peer(dz))
+            passes[p, n].start()
+
+    def slot(q, p):
+        at, rows = PARTS[p]
+        return done.at[pl.ds(pl.multiple_of(c * half + q * size + at, 8), rows)]
+
+    for p, (at, rows) in enumerate(PARTS):
+        for n in range(7):
+            passes[p, n].wait_recv()
+        total = z_buf[0, pl.ds(at, rows), :]
         for q in range(1, 8):
-            total = total + z_buf[q]
-
-    def slot(q):
-        return pl.ds(pl.multiple_of(c * half + q * size, size), size)
-
-    if STOP >= 7:
-        done[slot(me), :] = total
-        gathers, onward = [], []
+            total = total + z_buf[q, pl.ds(at, rows), :]
+        done[pl.ds(pl.multiple_of(c * half + me * size + at, 8), rows), :] = total
         for n, (dx, dy) in enumerate(XY_OFFSETS):
-            gathers.append(remote(done.at[slot(me)], done.at[slot(me)], gsend.at[n], grecv.at[n], xy_peer(dx, dy)[1]))
-            gathers[-1].start()
-        near = [(0, 0)] + [XY_OFFSETS[n] for n in range(14, -1, -1)]
+            gathers[p, n] = remote(slot(me, p), slot(me, p), gsend.at[p * 15 + n], grecv.at[p * 15 + n], xy_peer(dx, dy)[1])
+            gathers[p, n].start()
+    near = [(0, 0)] + [XY_OFFSETS[n] for n in range(14, -1, -1)]
+    for p in range(len(PARTS)):
         for n, (dx, dy) in enumerate(near):
             if n:
-                gathers[15 - n].wait_recv()
+                gathers[p, 15 - n].wait_recv()
             q = lax.rem(x - dx + 4, 4) * 4 + lax.rem(y - dy + 4, 4)
-            onward.append(remote(done.at[slot(q)], done.at[slot(q)], fsend.at[n], frecv.at[n], core_peer()))
-            onward[-1].start()
-        for move in onward:
-            move.wait_recv()
-        sent += gathers + onward
+            onward[p, n] = remote(slot(q, p), slot(q, p), fsend.at[p * 16 + n], frecv.at[p * 16 + n], core_peer())
+            onward[p, n].start()
+    for move in onward.values():
+        move.wait_recv()
+    sent += [*outs.values(), *passes.values(), *gathers.values(), *onward.values()]
 
     if STOP >= 8:
         for n, (i, j) in enumerate(BLOCKS):
@@ -336,8 +335,8 @@
             pltpu.VMEM((128, 512), F32),
             pltpu.VMEM((128, 128), F32),
             pltpu.VMEM((2, 128, 8, 128), F32),
-            DMA((2,)), DMA((30,)), DMA((30,)), DMA((1,)), DMA((1,)), DMA((15,)), DMA((15,)),
-            DMA((7,)), DMA((7,)), DMA((15,)), DMA((15,)), DMA((16,)), DMA((16,)),
+            DMA((2,)), DMA((30,)), DMA((30,)), DMA((1,)), DMA((1,)), DMA((30,)), DMA((30,)),
+            DMA((14,)), DMA((14,)), DMA((30,)), DMA((30,)), DMA((32,)), DMA((32,)),
             DMA((30,)), DMA((30,)), pltpu.SemaphoreType.REGULAR((3,)), DMA((1,)),
         ],
         compiler_params=pltpu.CompilerParams(collective_id=0, has_side_effects=True, vmem_limit_bytes=LIMIT),

time: 166 us -> 165 us (level)
  no operation moved by 1% of the time
where the time goes in v4:
time: 165 us
  Pallas kernels  162 us (98%)
  local copies, waits for them, and re-layouts  2.62 us (2%)
    pallas_call x1, Pallas kernels, on_device(): pl.pallas_call(kernel, out_shape=outs, in_specs=[ANY, ANY], out_specs=(VM...  162 us

profile of v4, /device:TPU:1, one launch (start us, length us, event | category | flops | bytes accessed | tf_op | source)
XLA Modules:
  0.0 164.9 jit_solution(7190192460258855473)
XLA Ops:
  0.6 0.0 copy-start
  0.6 0.9 copy-done
  1.6 161.7 %hosvd_mode.1 = (f32[512,128]{1,0:T(8,128)S(1)}, f32[8,8,32,128]{3,2,1,0:T(8,128)S(1)}) custom-call(f32[8,32,32,128]{3,2,1,0:T(8,128)} %snap.1, f32[512,128]{1,0:T(8,128)S(1)} %copy-done), custom_call_target="tpu_custom_call" | custom-call | tf_op jit(solution)/shard_map/hosvd_mode/pallas_call | solution.py:316
  163.3 0.7 copy.6
  164.0 1.0 copy.7
Async XLA Ops:
  0.6 1.0 copy-start

commit v5 on v4

--- a/solution.py
+++ b/solution.py
@@ -279,12 +279,13 @@
                 for dy in (2, 1, 3):
                     back(h, r * 4 + lax.rem(y + dy, 4), 6 + (h * 4 + r) * 3 + dy - 1, 6 + (h * 4 + zh) * 3 + dy - 1)
 
+        image[...] = dot(turned[...], gram[...], (1, 0), HIGHEST)
         for step in range(ITERS):
-            image[...] = dot(turned[...], gram[...], (1, 0), HIGHEST)
             small = dot(image[...], image[...], (1, 1), HIGHEST)
             if step < ITERS - 1:
+                ahead = dot(image[...], gram[...], (1, 0), HIGHEST)
                 triangular_inverse(small, inverse)
-                turned[...] = dot(inverse[...], image[...], (1, 0), HIGHEST)
+                image[...] = dot(inverse[...], ahead, (1, 0), HIGHEST)
             else:
                 triangular_inverse(small, inverse, ranks_done)
         for h in range(2):
@@ -310,10 +311,18 @@
 DMA = pltpu.SemaphoreType.DMA
 
 
+def finish(factor_in, core_in, factor, core, sems):
+    copies = [pltpu.make_async_copy(core_in, core, sems.at[0]), pltpu.make_async_copy(factor_in, factor, sems.at[1])]
+    for copy in copies:
+        copy.start()
+    for copy in copies:
+        copy.wait()
+
+
 def on_device(snapshot, start_factor):
     size = SLICE * 8
     outs = (jax.ShapeDtypeStruct((512, 128), F32), jax.ShapeDtypeStruct((8, 8, 32, 128), F32))
-    return pl.pallas_call(
+    results = pl.pallas_call(
         kernel,
         out_shape=outs,
         in_specs=[ANY, ANY],
@@ -342,6 +351,15 @@
         compiler_params=pltpu.CompilerParams(collective_id=0, has_side_effects=True, vmem_limit_bytes=LIMIT),
         name="hosvd_mode",
     )(snapshot, start_factor)
+    return pl.pallas_call(
+        finish,
+        out_shape=outs,
+        in_specs=[ANY, ANY],
+        out_specs=(ANY, ANY),
+        scratch_shapes=[DMA((2,))],
+        compiler_params=pltpu.CompilerParams(vmem_limit_bytes=2**20),
+        name="finish",
+    )(*results)
 
 
 def solution(mesh):

time: 165 us -> 164 us (level)
  local copies, waits for them, and re-layouts: 2.62 us -> 0.94 us
    unnamed x4 -> x2, local copies, waits for them, and re-layouts: 2.62 us -> 0.94 us
where the time goes in v5:
time: 164 us
  Pallas kernels  162 us (99%)
    pallas_call x1, Pallas kernels, on_device(): pl.pallas_call(kernel, out_shape=outs, in_specs=[ANY, ANY], out_specs=(VM...  161 us

profile of v5, /device:TPU:1, one launch (start us, length us, event | category | flops | bytes accessed | tf_op | source)
XLA Modules:
  0.0 164.0 jit_solution(6936171425056795222)
XLA Ops:
  0.6 0.0 copy-start
  0.6 0.9 copy-done
  1.6 161.2 %hosvd_mode.1 = (f32[512,128]{1,0:T(8,128)S(1)}, f32[8,8,32,128]{3,2,1,0:T(8,128)S(1)}) custom-call(f32[8,32,32,128]{3,2,1,0:T(8,128)} %snap.1, f32[512,128]{1,0:T(8,128)S(1)} %copy-done), custom_call_target="tpu_custom_call" | custom-call | tf_op jit(solution)/shard_map/hosvd_mode/pallas_call | solution.py:325
  162.8 1.1 finish.1
Async XLA Ops:
  0.6 1.0 copy-start

commit v6 on v5

--- a/solution.py
+++ b/solution.py
@@ -195,24 +195,24 @@
                             block = block + partial[pl.ds(n * 128, 128), :]
                         partial[pl.ds(n * 128, 128), :] = block
 
-    half = 80 * 8
-    if STOP >= 4:
-        swap = remote(partial.at[rows_of(1 - c, half)], core_buf, csend.at[0], crecv.at[0], core_peer())
-        swap.start()
-        sent.append(swap)
-        swap.wait_recv()
-        part[...] = partial[rows_of(c, half), :] + core_buf[...]
-
     size = SLICE * 8
+    half = 16 * size
     me = x * 4 + y
-    outs, passes, gathers, onward = {}, {}, {}, {}
+    swaps, outs, passes, gathers, onward = {}, {}, {}, {}, {}
+    halves = partial.reshape(32, size, 128)
     for p, (at, rows) in enumerate(PARTS):
+        piece = pl.ds(at, rows)
+        swaps[p] = remote(halves.at[rows_of(1 - c, 16), piece, :], core_buf.at[:, piece, :], csend.at[p], crecv.at[p], core_peer())
+        swaps[p].start()
+    for p, (at, rows) in enumerate(PARTS):
+        piece = pl.ds(at, rows)
+        swaps[p].wait_recv()
+        part[:, piece, :] = halves[rows_of(c, 16), piece, :] + core_buf[:, piece, :]
         for n, (dx, dy) in enumerate(XY_OFFSETS):
             q, device = xy_peer(dx, dy)
-            piece = part.at[pl.ds(pl.multiple_of(q * size + at, 8), rows)]
-            outs[p, n] = remote(piece, xy_buf.at[me, pl.ds(at, rows)], xsend.at[p * 15 + n], xrecv.at[p * 15 + n], device)
+            outs[p, n] = remote(part.at[q, piece], xy_buf.at[me, piece], xsend.at[p * 15 + n], xrecv.at[p * 15 + n], device)
             outs[p, n].start()
-    xy_buf[me] = part[rows_of(me, size), :]
+        xy_buf[me, piece, :] = part[me, piece, :]
     for p, (at, rows) in enumerate(PARTS):
         for n in range(15):
             outs[p, n].wait_recv()
@@ -247,16 +247,24 @@
             q = lax.rem(x - dx + 4, 4) * 4 + lax.rem(y - dy + 4, 4)
             onward[p, n] = remote(slot(q, p), slot(q, p), fsend.at[p * 16 + n], frecv.at[p * 16 + n], core_peer())
             onward[p, n].start()
+
+    def assemble(first):
+        for n, (i, j) in enumerate(BLOCKS):
+            if n // 5 == first:
+                block = done[pl.ds(n * 128, 128), :]
+                gram[pl.ds(i * 128, 128), pl.ds(j * 128, 128)] = block
+                if i != j:
+                    gram[pl.ds(j * 128, 128), pl.ds(i * 128, 128)] = block.T
+
+    for first in range(2):
+        pl.when(c == first)(functools.partial(assemble, first))
     for move in onward.values():
         move.wait_recv()
-    sent += [*outs.values(), *passes.values(), *gathers.values(), *onward.values()]
+    for first in range(2):
+        pl.when(c != first)(functools.partial(assemble, first))
+    sent += [*swaps.values(), *outs.values(), *passes.values(), *gathers.values(), *onward.values()]
 
     if STOP >= 8:
-        for n, (i, j) in enumerate(BLOCKS):
-            block = done[pl.ds(n * 128, 128), :]
-            gram[pl.ds(i * 128, 128), pl.ds(j * 128, 128)] = block
-            if i != j:
-                gram[pl.ds(j * 128, 128), pl.ds(i * 128, 128)] = block.T
         staged = stage.reshape(2 * 128 * 8, 128)
         backs = []
 
@@ -332,8 +340,8 @@
             pltpu.VMEM((2, 512, 1024), BF16),
             pltpu.VMEM((2, 512, 1024), BF16),
             pltpu.VMEM((1280, 128), F32),
-            pltpu.VMEM((640, 128), F32),
-            pltpu.VMEM((640, 128), F32),
+            pltpu.VMEM((16, size, 128), F32),
+            pltpu.VMEM((16, size, 128), F32),
             pltpu.VMEM((16, size, 128), F32),
             pltpu.VMEM((size, 128), F32),
             pltpu.VMEM((8, size, 128), F32),
@@ -344,7 +352,7 @@
             pltpu.VMEM((128, 512), F32),
             pltpu.VMEM((128, 128), F32),
             pltpu.VMEM((2, 128, 8, 128), F32),
-            DMA((2,)), DMA((30,)), DMA((30,)), DMA((1,)), DMA((1,)), DMA((30,)), DMA((30,)),
+            DMA((2,)), DMA((30,)), DMA((30,)), DMA((2,)), DMA((2,)), DMA((30,)), DMA((30,)),
             DMA((14,)), DMA((14,)), DMA((30,)), DMA((30,)), DMA((32,)), DMA((32,)),
             DMA((30,)), DMA((30,)), pltpu.SemaphoreType.REGULAR((3,)), DMA((1,)),
         ],

time: 164 us -> 164 us (level)
  no operation moved by 1% of the time
where the time goes in v6:
time: 164 us
  Pallas kernels  162 us (99%)
    pallas_call x1, Pallas kernels, on_device(): pl.pallas_call(kernel, out_shape=outs, in_specs=[ANY, ANY], out_specs=(VM...  161 us

profile of v6, /device:TPU:1, one launch (start us, length us, event | category | flops | bytes accessed | tf_op | source)
XLA Modules:
  0.0 164.1 jit_solution(3306724355509088398)
XLA Ops:
  0.6 0.0 copy-start
  0.6 0.9 copy-done
  1.6 161.3 %hosvd_mode.1 = (f32[512,128]{1,0:T(8,128)S(1)}, f32[8,8,32,128]{3,2,1,0:T(8,128)S(1)}) custom-call(f32[8,32,32,128]{3,2,1,0:T(8,128)} %snap.1, f32[512,128]{1,0:T(8,128)S(1)} %copy-done), custom_call_target="tpu_custom_call" | custom-call | tf_op jit(solution)/shard_map/hosvd_mode/pallas_call | solution.py:333
  162.8 1.1 finish.1
Async XLA Ops:
  0.6 1.0 copy-start
